TPU v7x, 32 devices: a whole 2x2x4 slice. The times are simulated.
32 devices in a mesh: blk: 8 (over z, x), tok: 4 (over y, core).
Axes of the slice: x: 2, y: 2, z: 4, core: 2. Of those that a mesh axis runs over, the one named last changes fastest.
Arguments:
- stream: bfloat16 [4096, 1664], P(('tok', 'blk'))
- queries: bfloat16 [4096, 1664], P(('tok', 'blk'))
- key_cache: bfloat16 [4096, 1664], P(('tok', 'blk'))
- value_cache: bfloat16 [4096, 1664], P(('tok', 'blk')), may hold values from -6 to 6
- segments: int32 [4096], P('tok'), may hold values from 63 to 4095, as said below
- stale_rows: int32 [384], P(('tok', 'blk')), may hold values from 0 to 4095, as said below
- owners: int32 [1024], P(('tok', 'blk')), may hold values from 0 to 3, as said below
- attn_gain: float32 [1664], replicated, may hold values from 0.1 to 1.9
- w_key: bfloat16 [1664, 1664], replicated, may hold values from -0.15625 to 0.15625
- key_bias: float32 [1664], replicated, may hold values from -3 to 3
- mlp_gain: float32 [1664], replicated, may hold values from 0.1 to 1.9
- w_fc: bfloat16 [1664, 8192], P(None, 'blk'), may hold values from -0.15625 to 0.15625
- b_fc: float32 [8192], P('blk'), may hold values from -3 to 3
- w_proj: bfloat16 [8192, 1664], P('blk'), may hold values from -0.125 to 0.125
- b_proj: float32 [1664], replicated, may hold values from -3 to 3
- merge_gain: float32 [1664], replicated, may hold values from 0.1 to 1.9
- w_merge: bfloat16 [1664, 1664], replicated, may hold values from -0.15625 to 0.15625
- b_merge: float32 [1664], replicated, may hold values from -3 to 3
Outputs:
- refreshed_keys: bfloat16 [4096, 1664], P(('tok', 'blk'))
- delivered: bfloat16 [4, 8, 128, 1664], P('tok', 'blk')
Inputs may be any that keep to these rules, and one draw needn't show every extreme that they name: `segments`: A segment's id is the index of its last row, so ids never fall; each segment has 4 to 128 rows, a multiple of 4, and lies inside one aligned block of 1024 rows; each such block begins with a segment of 64 rows followed by one of exactly 128 rows. `stale_rows`: Distinct; the aligned block of 128 rows of each device holds exactly 12 of them, all inside that block and listed on that device; row 0 and the last row are always listed. `owners`: all merged tokens of one segment (the segment of row 4 m for merged token m) have the same owner.
All inputs are finite; a program needn't handle non-finite values.
Results may differ from a plain program's by a relative error of at most 0.011.
Values may be sent and summed in bfloat16 or wider, within the bound.
A program may use at most 192 MiB of HBM per device.

v0:
```python
import functools

import jax
import jax.numpy as jnp
from jax import lax
from jax.experimental import pallas as pl
from jax.experimental.pallas import tpu as pltpu
from jax.sharding import PartitionSpec as P

HEADS = 16
MESH = pl.DeviceIdType.MESH


def layer_norm(values, gain):
    center = values - jnp.mean(values, axis=-1, keepdims=True)
    spread = jnp.mean(center * center, axis=-1, keepdims=True)
    return center * lax.rsqrt(spread + 1e-06) * gain


def pool_matrix(groups):
    rows = lax.broadcasted_iota(jnp.int32, (groups, groups * 4), 1)
    group = lax.broadcasted_iota(jnp.int32, (groups, groups * 4), 0) * 4
    inside = (rows >= group) & (rows < group + 4)
    return jnp.where(inside, 1.0, 0.0).astype(jnp.bfloat16)


def dot(a, b):
    return jnp.dot(a, b, preferred_element_type=jnp.float32)


def mlp_kernel(
    n,
    nt,
    stream_ref,
    query_ref,
    key_ref,
    value_ref,
    key_seg,
    query_seg,
    stale_row,
    stale_col,
    attn_gain,
    key_bias,
    owner_row,
    owner_col,
    mlp_gain,
    b_fc,
    b_proj,
    merge_gain,
    b_merge,
    w_key_hbm,
    w_fc_hbm,
    w_proj_hbm,
    w_merge_hbm,
    refreshed_ref,
    out_ref,
    keys,
    values,
    fresh,
    stale_near,
    probs,
    attended,
    att_ref,
    gath,
    w_key,
    w_fc,
    w_proj,
    w_merge,
    pooled_units,
    part,
    landed,
    total,
    outgoing,
    arrived,
    weight_sem,
    halo_send,
    halo_recv,
    ag_recv,
    up_send,
    down_send,
    cross_send,
    rs_send,
    rs_recv,
    out_send,
    out_recv,
):
    rows = stream_ref.shape[0]
    groups = rows // 4
    width = stream_ref.shape[1]
    units = b_fc.shape[1]
    line = n // 2
    blk = lax.axis_index("blk")
    tok = lax.axis_index("tok")
    lo = lax.rem(blk, 2)
    hi = lax.div(blk, 2)
    partner = blk + 1 - 2 * lo

    loads = [
        pltpu.make_async_copy(src, dst, weight_sem.at[k])
        for k, (src, dst) in enumerate(
            (
                (w_key_hbm, w_key),
                (w_fc_hbm, w_fc),
                (w_proj_hbm, w_proj),
                (w_merge_hbm, w_merge),
            )
        )
    ]
    for load in loads:
        load.start()

    barrier = pltpu.get_barrier_semaphore()
    for k in range(1, n):
        pl.semaphore_signal(
            barrier, inc=1, device_id={"blk": lax.rem(blk + k, n)}, device_id_type=MESH
        )
    for k in range(1, nt):
        pl.semaphore_signal(
            barrier, inc=1, device_id={"tok": lax.rem(tok + k, nt)}, device_id_type=MESH
        )
    head_size = width // HEADS
    has_below = blk > 0
    has_above = blk + 1 < n

    def halo_copy(kind, src, dst, side):
        target = blk + 1 if side == 0 else blk - 1
        return pltpu.make_async_remote_copy(
            src_ref=src,
            dst_ref=dst,
            send_sem=halo_send.at[kind, side],
            recv_sem=halo_recv.at[kind, side],
            device_id={"blk": target},
            device_id_type=MESH,
        )

    def halo(side, kind):
        src, dst = (
            (key_ref, keys.at[2 * side]),
            (stale_row, stale_near.at[side]),
            (fresh.at[2], fresh.at[side]),
            (value_ref, values.at[2 * side]),
        )[kind]
        return halo_copy(kind, src, dst, side)

    def for_sides(kinds, what, sending):
        for side in range(2):
            there = has_above if (side == 0) == sending else has_below

            @pl.when(there)
            def _(side=side):
                for kind in kinds:
                    getattr(halo(side, kind), what)()

    pl.semaphore_wait(barrier, n - 1 + nt - 1)
    for_sides((0, 1), "start", True)

    slot_count = stale_col.shape[0]
    rows_of_slot = lax.broadcasted_iota(jnp.int32, (slot_count, rows), 1)
    pick = jnp.where(rows_of_slot == stale_col[...], 1.0, 0.0).astype(jnp.bfloat16)
    held = layer_norm(dot(pick, stream_ref[...]), attn_gain[...]).astype(jnp.bfloat16)
    loads[0].wait()
    fresh[2] = (dot(held, w_key[...]) + key_bias[...]).astype(jnp.bfloat16)
    for_sides((2, 3), "start", True)

    def refresh(cache, stale, new_rows):
        row_ids = lax.broadcasted_iota(jnp.int32, (rows, slot_count), 0)
        spread = jnp.where(row_ids == stale[0:1, :slot_count], 1.0, 0.0)
        hit = jnp.sum(spread, axis=1, keepdims=True) > 0.5
        return jnp.where(
            hit, dot(spread.astype(jnp.bfloat16), new_rows), cache.astype(jnp.float32)
        ).astype(jnp.bfloat16)

    keys[1] = refresh(key_ref[...], stale_row[...], fresh[2])
    refreshed_ref[...] = keys[1]
    values[1] = value_ref[...]
    for side in range(2):

        @pl.when(jnp.logical_not(has_below if side == 0 else has_above))
        def _(side=side):
            keys[2 * side] = jnp.zeros((rows, width), jnp.bfloat16)
            values[2 * side] = jnp.zeros((rows, width), jnp.bfloat16)

        @pl.when(has_below if side == 0 else has_above)
        def _(side=side):
            for kind in range(3):
                halo(side, kind).wait_recv()
            keys[2 * side] = refresh(keys[2 * side], stale_near[side], fresh[side])

    allowed = query_seg[...] == key_seg[...]

    def window(head):
        first = head * head_size // 128 * 128
        last = min(first + 256, width)
        lane = lax.broadcasted_iota(jnp.int32, (rows, last - first), 1) + first
        mine = (lane >= head * head_size) & (lane < (head + 1) * head_size)
        return slice(first, last), mine

    for head in range(HEADS):
        cols, mine = window(head)
        query = jnp.where(mine, query_ref[:, cols].astype(jnp.float32), 0.0).astype(jnp.bfloat16)
        near = keys[:, :, cols].reshape(3 * rows, cols.stop - cols.start)
        scores = lax.dot_general(
            query, near, (((1,), (1,)), ((), ())), preferred_element_type=jnp.float32
        ) * (1.0 / head_size**0.5)
        scores = jnp.where(allowed, scores, -jnp.inf)
        weights = jnp.exp(scores - jnp.max(scores, axis=-1, keepdims=True))
        probs[head] = (weights / jnp.sum(weights, axis=-1, keepdims=True)).astype(jnp.bfloat16)

    for_sides((3,), "wait_recv", False)
    attended[...] = jnp.zeros_like(attended)
    for head in range(HEADS):
        cols, mine = window(head)
        near = values[:, :, cols].reshape(3 * rows, cols.stop - cols.start)
        attended[:, cols] += jnp.where(mine, dot(probs[head], near), 0.0)
    att_ref[...] = attended[...].astype(jnp.bfloat16)
    mixed = stream_ref[...].astype(jnp.float32) + att_ref[...].astype(jnp.float32)
    gath[blk] = layer_norm(mixed, mlp_gain[...]).astype(jnp.bfloat16)

    def passed(block, target, sems):
        return pltpu.make_async_remote_copy(
            src_ref=gath.at[block],
            dst_ref=gath.at[block],
            send_sem=sems.at[block],
            recv_sem=ag_recv.at[block],
            device_id={"blk": target},
            device_id_type=MESH,
        )

    def partial_copy(block):
        return pltpu.make_async_remote_copy(
            src_ref=part.at[block],
            dst_ref=landed.at[blk],
            send_sem=rs_send.at[block],
            recv_sem=rs_recv.at[blk],
            device_id={"blk": block},
            device_id_type=MESH,
        )

    def got(block):
        passed(block, partner, cross_send).wait_recv()

    @pl.when(hi + 1 < line)
    def _():
        passed(blk, blk + 2, up_send).start()

    @pl.when(hi > 0)
    def _():
        passed(blk, blk - 2, down_send).start()

    passed(blk, partner, cross_send).start()
    loads[1].wait()
    loads[2].wait()
    pool = pool_matrix(2 * groups)
    chunk = min(units, 256)

    def work(pair):
        block_rows = gath[pl.ds(2 * pair, 2)].reshape(2 * rows, width)
        for k in range(units // chunk):
            cols = slice(k * chunk, (k + 1) * chunk)
            pre = dot(block_rows, w_fc[:, cols]) + b_fc[:, cols]
            act = (0.5 * pre * (1.0 + lax.erf(pre * 0.7071067811865476))).astype(jnp.bfloat16)
            pooled_units[:, cols] = dot(pool, act).astype(jnp.bfloat16)
        result = dot(pooled_units[...], w_proj[...]).astype(jnp.bfloat16)
        for k in range(2):
            part[2 * pair + k] = result[k * groups : (k + 1) * groups]
        for k in range(2):
            block = 2 * pair + k

            @pl.when(block != blk)
            def _(block=block):
                partial_copy(block).start()

    def step(s, carry):
        below = hi - s
        above = hi + s

        @pl.when((s < line) & (below >= 0))
        def _():
            block = 2 * below + lo
            got(block)

            @pl.when(hi + 1 < line)
            def _():
                passed(block, blk + 2, up_send).start()

            passed(block, partner, cross_send).start()

        @pl.when((s < line) & (above < line))
        def _():
            block = 2 * above + lo
            got(block)

            @pl.when(hi > 0)
            def _():
                passed(block, blk - 2, down_send).start()

            passed(block, partner, cross_send).start()

        def side(d, inner):
            pair = hi + (2 * d - 1) * (s - 1)

            @pl.when((pair >= 0) & (pair < line) & ((d == 0) | (s > 1)))
            def _():
                got(2 * pair + 1 - lo)
                work(pair)

            return inner

        return lax.fori_loop(0, 2, side, carry)

    lax.fori_loop(1, line + 1, step, 0)

    total[...] = part[blk].astype(jnp.float32)

    def collect(k, carry):
        source = lax.rem(blk + k, n)
        pltpu.make_async_remote_copy(
            src_ref=part.at[source],
            dst_ref=landed.at[source],
            send_sem=rs_send.at[source],
            recv_sem=rs_recv.at[source],
            device_id={"blk": source},
            device_id_type=MESH,
        ).wait_recv()
        total[...] += landed[source].astype(jnp.float32)
        return carry

    lax.fori_loop(1, n, collect, 0)
    pool_own = pool_matrix(groups)
    own = dot(pool_own, stream_ref[...]) + dot(pool_own, att_ref[...])
    pooled = (own + total[...]) * 0.25 + b_proj[...]
    merge_in = layer_norm(pooled, merge_gain[...]).astype(jnp.bfloat16)
    loads[3].wait()
    merged = (dot(merge_in, w_merge[...]) + b_merge[...]).astype(jnp.bfloat16)
    first = lax.broadcasted_iota(jnp.int32, (groups, groups), 0)
    second = lax.broadcasted_iota(jnp.int32, (groups, groups), 1)
    same = (owner_col[...] == owner_row[...]) & (first < second)
    ranking = jnp.sum(jnp.where(same, 1.0, 0.0), axis=0, keepdims=True).astype(jnp.int32)
    place = owner_row[...] * groups + ranking
    slots = lax.broadcasted_iota(jnp.int32, (nt * groups, groups), 0)
    selector = jnp.where(slots == place, 1.0, 0.0).astype(jnp.bfloat16)
    outgoing[...] = dot(selector, merged).astype(jnp.bfloat16).reshape(nt, groups, width)

    def delivery(owner, source):
        return pltpu.make_async_remote_copy(
            src_ref=outgoing.at[owner],
            dst_ref=arrived.at[source],
            send_sem=out_send.at[owner],
            recv_sem=out_recv.at[source],
            device_id={"tok": owner},
            device_id_type=MESH,
        )

    for k in range(1, nt):
        delivery(lax.rem(tok + k, nt), tok).start()
    out_ref[tok] = outgoing[tok]

    def settle(j, carry):
        block = 2 * j + lo

        @pl.when((j <= hi) & (hi + 1 < line))
        def _():
            passed(block, blk + 2, up_send).wait_send()

        @pl.when((j >= hi) & (hi > 0))
        def _():
            passed(block, blk - 2, down_send).wait_send()

        passed(block, partner, cross_send).wait_send()
        return carry

    lax.fori_loop(0, line, settle, 0)
    for_sides((0, 1, 2, 3), "wait_send", True)

    def settle_partial(k, carry):
        partial_copy(lax.rem(blk + k, n)).wait_send()
        return carry

    lax.fori_loop(1, n, settle_partial, 0)
    for k in range(1, nt):
        other = lax.rem(tok + k, nt)
        delivery(other, other).wait_recv()
        out_ref[other] = arrived[other]
    for k in range(1, nt):
        delivery(lax.rem(tok + k, nt), tok).wait_send()


def block_kernel(
    stream,
    queries,
    key_cache,
    value_cache,
    key_seg,
    query_seg,
    stale,
    owners,
    attn_gain,
    w_key,
    key_bias,
    mlp_gain,
    w_fc,
    b_fc,
    w_proj,
    b_proj,
    merge_gain,
    w_merge,
    b_merge,
):
    n, nt = lax.axis_size("blk"), lax.axis_size("tok")
    rows, width = stream.shape
    groups = rows // 4
    units = w_fc.shape[1]
    slot_count = -(-stale.shape[0] // 16) * 16
    stale_lanes = jnp.pad(stale, (0, 128 - stale.shape[0]), constant_values=-1)
    vmem = pl.BlockSpec(memory_space=pltpu.VMEM)
    hbm = pl.BlockSpec(memory_space=pl.ANY)
    return pl.pallas_call(
        functools.partial(mlp_kernel, n, nt),
        out_shape=(
            jax.ShapeDtypeStruct((rows, width), jnp.bfloat16),
            jax.ShapeDtypeStruct((nt, groups, width), jnp.bfloat16),
        ),
        in_specs=[vmem] * 17 + [hbm] * 4,
        out_specs=(vmem, vmem),
        scratch_shapes=[
            pltpu.VMEM((3, rows, width), jnp.bfloat16),
            pltpu.VMEM((3, rows, width), jnp.bfloat16),
            pltpu.VMEM((3, slot_count, width), jnp.bfloat16),
            pltpu.VMEM((2, 8, 128), jnp.int32),
            pltpu.VMEM((HEADS, rows, 3 * rows), jnp.bfloat16),
            pltpu.VMEM((rows, width), jnp.float32),
            pltpu.VMEM((rows, width), jnp.bfloat16),
            pltpu.VMEM((n, rows, width), jnp.bfloat16),
            pltpu.VMEM(w_key.shape, jnp.bfloat16),
            pltpu.VMEM(w_fc.shape, jnp.bfloat16),
            pltpu.VMEM(w_proj.shape, jnp.bfloat16),
            pltpu.VMEM(w_merge.shape, jnp.bfloat16),
            pltpu.VMEM((2 * groups, units), jnp.bfloat16),
            pltpu.VMEM((n, groups, width), jnp.bfloat16),
            pltpu.VMEM((n, groups, width), jnp.bfloat16),
            pltpu.VMEM((groups, width), jnp.float32),
            pltpu.VMEM((nt, groups, width), jnp.bfloat16),
            pltpu.VMEM((nt, groups, width), jnp.bfloat16),
            pltpu.SemaphoreType.DMA((4,)),
            pltpu.SemaphoreType.DMA((4, 2)),
            pltpu.SemaphoreType.DMA((4, 2)),
            pltpu.SemaphoreType.DMA((n,)),
            pltpu.SemaphoreType.DMA((n,)),
            pltpu.SemaphoreType.DMA((n,)),
            pltpu.SemaphoreType.DMA((n,)),
            pltpu.SemaphoreType.DMA((n,)),
            pltpu.SemaphoreType.DMA((n,)),
            pltpu.SemaphoreType.DMA((nt,)),
            pltpu.SemaphoreType.DMA((nt,)),
        ],
        compiler_params=pltpu.CompilerParams(
            collective_id=1, has_side_effects=True, vmem_limit_bytes=56 * 1024 * 1024
        ),
    )(
        stream,
        queries,
        key_cache,
        value_cache,
        key_seg.reshape(1, 3 * rows),
        query_seg.reshape(rows, 1),
        jnp.broadcast_to(stale_lanes[None, :], (8, 128)),
        stale_lanes[:slot_count].reshape(slot_count, 1),
        attn_gain.reshape(1, width),
        key_bias.reshape(1, width),
        owners.reshape(1, groups),
        owners.reshape(groups, 1),
        mlp_gain.reshape(1, width),
        b_fc.reshape(1, units),
        b_proj.reshape(1, width),
        merge_gain.reshape(1, width),
        b_merge.reshape(1, width),
        w_key,
        w_fc,
        w_proj,
        w_merge,
    )


def body(
    stream,
    queries,
    key_cache,
    value_cache,
    segments,
    stale_rows,
    owners,
    attn_gain,
    w_key,
    key_bias,
    mlp_gain,
    w_fc,
    b_fc,
    w_proj,
    b_proj,
    merge_gain,
    w_merge,
    b_merge,
):
    row_count = stream.shape[0]
    model_width = stream.shape[1]
    local_rows = stale_rows % row_count
    position = lax.axis_index("blk")
    minus_ones = jnp.full((row_count,), -1, jnp.int32)
    seg_padded = jnp.concatenate([minus_ones, segments, minus_ones], axis=0)
    key_seg = lax.dynamic_slice_in_dim(seg_padded, position * row_count, 3 * row_count, 0)
    query_seg = lax.dynamic_slice_in_dim(segments, position * row_count, row_count, 0)
    refreshed, arrived = block_kernel(
        stream,
        queries,
        key_cache,
        value_cache,
        key_seg,
        query_seg,
        local_rows,
        owners,
        attn_gain,
        w_key,
        key_bias,
        mlp_gain,
        w_fc,
        b_fc,
        w_proj,
        b_proj,
        merge_gain,
        w_merge,
        b_merge,
    )
    return (refreshed, arrived.reshape(1, 1, row_count, model_width))


def solution(mesh):
    return jax.shard_map(
        body,
        mesh=mesh,
        in_specs=(
            P(("tok", "blk"), None),
            P(("tok", "blk"), None),
            P(("tok", "blk"), None),
            P(("tok", "blk"), None),
            P("tok"),
            P(("tok", "blk")),
            P(("tok", "blk")),
            P(),
            P(),
            P(),
            P(),
            P(None, "blk"),
            P("blk"),
            P("blk", None),
            P(),
            P(),
            P(),
            P(),
        ),
        out_specs=(P(("tok", "blk"), None), P("tok", "blk", None, None)),
        check_vma=False,
    )
```

profile of v0, /device:TPU:27, one launch (start us, length us, event | category | flops | bytes accessed | tf_op | source)
XLA Modules:
  0.0 132.2 jit_solution(2320411220329047549)
XLA Ops:
  0.6 0.8 dynamic-slice_bitcast_fusion
  1.4 0.7 and_select_fusion
  2.1 0.8 fusion.1
  2.9 0.6 reshape.44.key_seg
  3.5 0.6 broadcast_in_dim.10.stale_row
  4.1 1.3 reshape.47.attn_gain
  5.3 1.3 reshape.48.key_bias
  6.6 1.3 reshape.51.mlp_gain
  7.9 1.3 reshape.53.b_proj
  9.2 1.3 reshape.54.merge_gain
  10.5 1.3 reshape.55.b_merge
  11.8 0.7 copy.21.stale_col
  12.5 1.3 %copy.22.owner_col = s32[32,1]{1,0:T(8,128)} copy(s32[32,1]{0,1:T(1,128)} %bitcast.10) | data formatting | bytes 256 | tf_op jit(solution)/shard_map/reshape | solution.py:471
  13.8 0.7 copy.20.query_seg
  14.6 114.0 %shard_map.185 = (bf16[128,1664]{1,0:T(8,128)(2,1)}, bf16[4,32,1664]{2,1,0:T(8,128)(2,1)}) custom-call(bf16[128,1664]{1,0:T(8,128)(2,1)} %stream_ref.1, bf16[128,1664]{1,0:T(8,128)(2,1)} %query_ref.1, bf16[128,1664]{1,0:T(8,128)(2,1)} %key_ref.1, bf16[128,1664]{1,0:T(8,128)(2,1)} %value_ref.1, s32[1,384]{1,0:T(1,128)} %reshape.44.key_seg, ...), custom_call_target="tpu_custom_call" | custom-call | tf_op jit(solution)/shard_map/pallas_call | solution.py:417
  128.6 1.8 %copy.25 = bf16[128,1664]{1,0:T(8,128)(2,1)} copy(bf16[128,1664]{1,0:T(8,128)(2,1)} %get-tuple-element.8) | data formatting | bytes 851968
  130.4 1.8 %copy.26 = bf16[1,1,128,1664]{3,2,1,0:T(8,128)(2,1)} copy(bf16[1,1,128,1664]{3,2,1,0:T(8,128)(2,1)} %bitcast.8) | data formatting | bytes 851968
  (3 shorter events, 0.0 us)
where the time goes:
time: 133 us; the launch traced here: 132 us
  Pallas kernels  114 us (86%)
  local copies, waits for them, and re-layouts  16.1 us (12%)
  other arithmetic  1.44 us (1%)
    pallas_call x1, Pallas kernels, block_kernel(): pl.pallas_call(functools.partial(mlp_kernel, n, nt), out_shape=(jax.Shape...  114 us
    unnamed x2, local copies, waits for them, and re-layouts  3.59 us

commit v1 on v0

--- a/solution.py
+++ b/solution.py
@@ -22,6 +22,14 @@
     group = lax.broadcasted_iota(jnp.int32, (groups, groups * 4), 0) * 4
     inside = (rows >= group) & (rows < group + 4)
     return jnp.where(inside, 1.0, 0.0).astype(jnp.bfloat16)
+
+
+def column(row):
+    size = row.shape[1]
+    first = lax.broadcasted_iota(jnp.int32, (size, size), 0)
+    second = lax.broadcasted_iota(jnp.int32, (size, size), 1)
+    spread = jnp.where(first == second, row.astype(jnp.float32), 0.0)
+    return jnp.sum(spread, axis=1, keepdims=True).astype(jnp.int32)
 
 
 def dot(a, b):
@@ -35,19 +43,14 @@
     query_ref,
     key_ref,
     value_ref,
-    key_seg,
-    query_seg,
-    stale_row,
-    stale_col,
-    attn_gain,
-    key_bias,
-    owner_row,
-    owner_col,
-    mlp_gain,
-    b_fc,
-    b_proj,
-    merge_gain,
-    b_merge,
+    index_ref,
+    attn_gain_ref,
+    key_bias_ref,
+    mlp_gain_ref,
+    b_fc_ref,
+    b_proj_ref,
+    merge_gain_ref,
+    b_merge_ref,
     w_key_hbm,
     w_fc_hbm,
     w_proj_hbm,
@@ -87,8 +90,26 @@
     rows = stream_ref.shape[0]
     groups = rows // 4
     width = stream_ref.shape[1]
-    units = b_fc.shape[1]
+    units = b_fc_ref.shape[0]
     line = n // 2
+    attn_gain, key_bias, mlp_gain, b_fc, b_proj, merge_gain, b_merge = (
+        ref[...].reshape(1, ref.shape[0])
+        for ref in (
+            attn_gain_ref,
+            key_bias_ref,
+            mlp_gain_ref,
+            b_fc_ref,
+            b_proj_ref,
+            merge_gain_ref,
+            b_merge_ref,
+        )
+    )
+    key_seg = jnp.concatenate([index_ref[k : k + 1, :rows] for k in range(3)], axis=1)
+    query_seg = column(index_ref[1:2, :rows])
+    slot_count = fresh.shape[1]
+    stale_col = column(index_ref[3:4, :slot_count])
+    owner_row = index_ref[4:5, :groups]
+    owner_col = column(owner_row)
     blk = lax.axis_index("blk")
     tok = lax.axis_index("tok")
     lo = lax.rem(blk, 2)
@@ -136,7 +157,7 @@
     def halo(side, kind):
         src, dst = (
             (key_ref, keys.at[2 * side]),
-            (stale_row, stale_near.at[side]),
+            (index_ref, stale_near.at[side]),
             (fresh.at[2], fresh.at[side]),
             (value_ref, values.at[2 * side]),
         )[kind]
@@ -154,23 +175,22 @@
     pl.semaphore_wait(barrier, n - 1 + nt - 1)
     for_sides((0, 1), "start", True)
 
-    slot_count = stale_col.shape[0]
     rows_of_slot = lax.broadcasted_iota(jnp.int32, (slot_count, rows), 1)
-    pick = jnp.where(rows_of_slot == stale_col[...], 1.0, 0.0).astype(jnp.bfloat16)
-    held = layer_norm(dot(pick, stream_ref[...]), attn_gain[...]).astype(jnp.bfloat16)
+    pick = jnp.where(rows_of_slot == stale_col, 1.0, 0.0).astype(jnp.bfloat16)
+    held = layer_norm(dot(pick, stream_ref[...]), attn_gain).astype(jnp.bfloat16)
     loads[0].wait()
-    fresh[2] = (dot(held, w_key[...]) + key_bias[...]).astype(jnp.bfloat16)
+    fresh[2] = (dot(held, w_key[...]) + key_bias).astype(jnp.bfloat16)
     for_sides((2, 3), "start", True)
 
     def refresh(cache, stale, new_rows):
         row_ids = lax.broadcasted_iota(jnp.int32, (rows, slot_count), 0)
-        spread = jnp.where(row_ids == stale[0:1, :slot_count], 1.0, 0.0)
+        spread = jnp.where(row_ids == stale[3:4, :slot_count], 1.0, 0.0)
         hit = jnp.sum(spread, axis=1, keepdims=True) > 0.5
         return jnp.where(
             hit, dot(spread.astype(jnp.bfloat16), new_rows), cache.astype(jnp.float32)
         ).astype(jnp.bfloat16)
 
-    keys[1] = refresh(key_ref[...], stale_row[...], fresh[2])
+    keys[1] = refresh(key_ref[...], index_ref[...], fresh[2])
     refreshed_ref[...] = keys[1]
     values[1] = value_ref[...]
     for side in range(2):
@@ -186,7 +206,7 @@
                 halo(side, kind).wait_recv()
             keys[2 * side] = refresh(keys[2 * side], stale_near[side], fresh[side])
 
-    allowed = query_seg[...] == key_seg[...]
+    allowed = query_seg == key_seg
 
     def window(head):
         first = head * head_size // 128 * 128
@@ -214,7 +234,7 @@
         attended[:, cols] += jnp.where(mine, dot(probs[head], near), 0.0)
     att_ref[...] = attended[...].astype(jnp.bfloat16)
     mixed = stream_ref[...].astype(jnp.float32) + att_ref[...].astype(jnp.float32)
-    gath[blk] = layer_norm(mixed, mlp_gain[...]).astype(jnp.bfloat16)
+    gath[blk] = layer_norm(mixed, mlp_gain).astype(jnp.bfloat16)
 
     def passed(block, target, sems):
         return pltpu.make_async_remote_copy(
@@ -328,15 +348,15 @@
     lax.fori_loop(1, n, collect, 0)
     pool_own = pool_matrix(groups)
     own = dot(pool_own, stream_ref[...]) + dot(pool_own, att_ref[...])
-    pooled = (own + total[...]) * 0.25 + b_proj[...]
-    merge_in = layer_norm(pooled, merge_gain[...]).astype(jnp.bfloat16)
+    pooled = (own + total[...]) * 0.25 + b_proj
+    merge_in = layer_norm(pooled, merge_gain).astype(jnp.bfloat16)
     loads[3].wait()
-    merged = (dot(merge_in, w_merge[...]) + b_merge[...]).astype(jnp.bfloat16)
+    merged = (dot(merge_in, w_merge[...]) + b_merge).astype(jnp.bfloat16)
     first = lax.broadcasted_iota(jnp.int32, (groups, groups), 0)
     second = lax.broadcasted_iota(jnp.int32, (groups, groups), 1)
-    same = (owner_col[...] == owner_row[...]) & (first < second)
+    same = (owner_col == owner_row) & (first < second)
     ranking = jnp.sum(jnp.where(same, 1.0, 0.0), axis=0, keepdims=True).astype(jnp.int32)
-    place = owner_row[...] * groups + ranking
+    place = owner_row * groups + ranking
     slots = lax.broadcasted_iota(jnp.int32, (nt * groups, groups), 0)
     selector = jnp.where(slots == place, 1.0, 0.0).astype(jnp.bfloat16)
     outgoing[...] = dot(selector, merged).astype(jnp.bfloat16).reshape(nt, groups, width)
@@ -390,10 +410,8 @@
     queries,
     key_cache,
     value_cache,
-    key_seg,
-    query_seg,
-    stale,
-    owners,
+    index,
+    slot_count,
     attn_gain,
     w_key,
     key_bias,
@@ -410,8 +428,6 @@
     rows, width = stream.shape
     groups = rows // 4
     units = w_fc.shape[1]
-    slot_count = -(-stale.shape[0] // 16) * 16
-    stale_lanes = jnp.pad(stale, (0, 128 - stale.shape[0]), constant_values=-1)
     vmem = pl.BlockSpec(memory_space=pltpu.VMEM)
     hbm = pl.BlockSpec(memory_space=pl.ANY)
     return pl.pallas_call(
@@ -420,7 +436,7 @@
             jax.ShapeDtypeStruct((rows, width), jnp.bfloat16),
             jax.ShapeDtypeStruct((nt, groups, width), jnp.bfloat16),
         ),
-        in_specs=[vmem] * 17 + [hbm] * 4,
+        in_specs=[vmem] * 12 + [hbm] * 4,
         out_specs=(vmem, vmem),
         scratch_shapes=[
             pltpu.VMEM((3, rows, width), jnp.bfloat16),
@@ -461,19 +477,14 @@
         queries,
         key_cache,
         value_cache,
-        key_seg.reshape(1, 3 * rows),
-        query_seg.reshape(rows, 1),
-        jnp.broadcast_to(stale_lanes[None, :], (8, 128)),
-        stale_lanes[:slot_count].reshape(slot_count, 1),
-        attn_gain.reshape(1, width),
-        key_bias.reshape(1, width),
-        owners.reshape(1, groups),
-        owners.reshape(groups, 1),
-        mlp_gain.reshape(1, width),
-        b_fc.reshape(1, units),
-        b_proj.reshape(1, width),
-        merge_gain.reshape(1, width),
-        b_merge.reshape(1, width),
+        index,
+        attn_gain,
+        key_bias,
+        mlp_gain,
+        b_fc,
+        b_proj,
+        merge_gain,
+        b_merge,
         w_key,
         w_fc,
         w_proj,
@@ -503,21 +514,34 @@
 ):
     row_count = stream.shape[0]
     model_width = stream.shape[1]
-    local_rows = stale_rows % row_count
     position = lax.axis_index("blk")
-    minus_ones = jnp.full((row_count,), -1, jnp.int32)
-    seg_padded = jnp.concatenate([minus_ones, segments, minus_ones], axis=0)
-    key_seg = lax.dynamic_slice_in_dim(seg_padded, position * row_count, 3 * row_count, 0)
-    query_seg = lax.dynamic_slice_in_dim(segments, position * row_count, row_count, 0)
+    blocks = lax.axis_size("blk")
+    edged = jnp.pad(
+        segments.reshape(blocks, row_count), ((1, 1), (0, 0)), constant_values=-1
+    )
+    segs = lax.dynamic_slice(edged, (position, 0), (3, row_count))
+    lanes = -(-row_count // 128) * 128
+
+    def widened(line):
+        return jnp.pad(line, ((0, 0), (0, lanes - line.shape[1])), constant_values=-1)
+
+    index = jnp.concatenate(
+        [
+            widened(segs),
+            widened((stale_rows % row_count)[None]),
+            widened(owners[None]),
+            jnp.full((3, lanes), -1, jnp.int32),
+        ],
+        axis=0,
+    )
+    slot_count = -(-stale_rows.shape[0] // 16) * 16
     refreshed, arrived = block_kernel(
         stream,
         queries,
         key_cache,
         value_cache,
-        key_seg,
-        query_seg,
-        local_rows,
-        owners,
+        index,
+        slot_count,
         attn_gain,
         w_key,
         key_bias,

time: 133 us -> 121 us (0.910)
  local copies, waits for them, and re-layouts: 16.1 us -> 4.36 us
    reshape x12 -> x0, local copies, waits for them, and re-layouts: 11.9 us -> none  [the longest x2 1.5 us: block_kernel(): query_seg.reshape(rows, 1)]
where the time goes in v1:
time: 121 us
  Pallas kernels  114 us (94%)
  local copies, waits for them, and re-layouts  4.36 us (4%)
  other arithmetic  1.98 us (2%)
    pallas_call x1, Pallas kernels, block_kernel(): pl.pallas_call(functools.partial(mlp_kernel, n, nt), out_shape=(jax.Shape...  114 us
    unnamed x2, local copies, waits for them, and re-layouts  3.59 us

profile of v1, /device:TPU:27, one launch (start us, length us, event | category | flops | bytes accessed | tf_op | source)
XLA Modules:
  0.0 121.1 jit_solution(15654007369511384649)
XLA Ops:
  0.6 0.7 fusion.3
  1.3 0.1 pad.18.clone
  1.4 0.7 pad_dynamic-slice_fusion
  2.1 1.3 %fusion.index_ref = s32[8,128]{1,0:T(8,128)} fusion(s32[1,32]{1,0:T(1,128)} %bitcast.7, s32[1,12]{1,0:T(1,128)S(1)} %fusion.3, s32[3,128]{1,0:T(4,128)S(1)} %pad_dynamic-slice_fusion, s32[8]{0:T(128)S(1)} %pad.18.clone), kind=kLoop, calls=%fused_computation.6 | loop fusion | flops 11264 | bytes 5840 | tf_op jit(solution)/shard_map/concatenate | solution.py:528
  3.4 114.1 %shard_map.185 = (bf16[128,1664]{1,0:T(8,128)(2,1)}, bf16[4,32,1664]{2,1,0:T(8,128)(2,1)}) custom-call(bf16[128,1664]{1,0:T(8,128)(2,1)} %stream_ref.1, bf16[128,1664]{1,0:T(8,128)(2,1)} %query_ref.1, bf16[128,1664]{1,0:T(8,128)(2,1)} %key_ref.1, bf16[128,1664]{1,0:T(8,128)(2,1)} %value_ref.1, s32[8,128]{1,0:T(8,128)} %fusion.index_ref, f32[1664]{0:T(1024)} %attn_gain_ref.1, ...), custom_call_target="tpu_custom_call" | custom-call | tf_op jit(solution)/shard_map/pallas_call | solution.py:433
  117.5 1.8 %copy.22 = bf16[128,1664]{1,0:T(8,128)(2,1)} copy(bf16[128,1664]{1,0:T(8,128)(2,1)} %get-tuple-element.8) | data formatting | bytes 851968
  119.3 1.8 %copy.23 = bf16[1,1,128,1664]{3,2,1,0:T(8,128)(2,1)} copy(bf16[1,1,128,1664]{3,2,1,0:T(8,128)(2,1)} %bitcast.5) | data formatting | bytes 851968
  (1 shorter events, 0.0 us)

commit v2 on v1

--- a/solution.py
+++ b/solution.py
@@ -226,12 +226,22 @@
         weights = jnp.exp(scores - jnp.max(scores, axis=-1, keepdims=True))
         probs[head] = (weights / jnp.sum(weights, axis=-1, keepdims=True)).astype(jnp.bfloat16)
 
-    for_sides((3,), "wait_recv", False)
     attended[...] = jnp.zeros_like(attended)
-    for head in range(HEADS):
-        cols, mine = window(head)
-        near = values[:, :, cols].reshape(3 * rows, cols.stop - cols.start)
-        attended[:, cols] += jnp.where(mine, dot(probs[head], near), 0.0)
+
+    def attend(slot):
+        for head in range(HEADS):
+            cols, mine = window(head)
+            share = probs[head, :, slot * rows : (slot + 1) * rows]
+            attended[:, cols] += jnp.where(mine, dot(share, values[slot, :, cols]), 0.0)
+
+    attend(1)
+    for side in range(2):
+
+        @pl.when(has_below if side == 0 else has_above)
+        def _(side=side):
+            halo(side, 3).wait_recv()
+            attend(2 * side)
+
     att_ref[...] = attended[...].astype(jnp.bfloat16)
     mixed = stream_ref[...].astype(jnp.float32) + att_ref[...].astype(jnp.float32)
     gath[blk] = layer_norm(mixed, mlp_gain).astype(jnp.bfloat16)
@@ -270,17 +280,23 @@
     passed(blk, partner, cross_send).start()
     loads[1].wait()
     loads[2].wait()
-    pool = pool_matrix(2 * groups)
+    pool = pool_matrix(groups)
     chunk = min(units, 256)
 
-    def work(pair):
-        block_rows = gath[pl.ds(2 * pair, 2)].reshape(2 * rows, width)
+    def half(pair, side):
+        block_rows = gath[2 * pair + side]
         for k in range(units // chunk):
             cols = slice(k * chunk, (k + 1) * chunk)
             pre = dot(block_rows, w_fc[:, cols]) + b_fc[:, cols]
             act = (0.5 * pre * (1.0 + lax.erf(pre * 0.7071067811865476))).astype(jnp.bfloat16)
-            pooled_units[:, cols] = dot(pool, act).astype(jnp.bfloat16)
-        result = dot(pooled_units[...], w_proj[...]).astype(jnp.bfloat16)
+            pooled_units[side, :, cols] = dot(pool, act).astype(jnp.bfloat16)
+
+    def work(pair):
+        half(pair, lo)
+        got(2 * pair + 1 - lo)
+        half(pair, 1 - lo)
+        both = pooled_units[...].reshape(2 * groups, units)
+        result = dot(both, w_proj[...]).astype(jnp.bfloat16)
         for k in range(2):
             part[2 * pair + k] = result[k * groups : (k + 1) * groups]
         for k in range(2):
@@ -321,7 +337,6 @@
 
             @pl.when((pair >= 0) & (pair < line) & ((d == 0) | (s > 1)))
             def _():
-                got(2 * pair + 1 - lo)
                 work(pair)
 
             return inner
@@ -451,7 +466,7 @@
             pltpu.VMEM(w_fc.shape, jnp.bfloat16),
             pltpu.VMEM(w_proj.shape, jnp.bfloat16),
             pltpu.VMEM(w_merge.shape, jnp.bfloat16),
-            pltpu.VMEM((2 * groups, units), jnp.bfloat16),
+            pltpu.VMEM((2, groups, units), jnp.bfloat16),
             pltpu.VMEM((n, groups, width), jnp.bfloat16),
             pltpu.VMEM((n, groups, width), jnp.bfloat16),
             pltpu.VMEM((groups, width), jnp.float32),

time: 121 us -> 122 us (level)
  no operation moved by 1% of the time
where the time goes in v2:
time: 122 us; the launch traced here: 121 us
  Pallas kernels  114 us (93%)
  local copies, waits for them, and re-layouts  4.36 us (4%)
  other arithmetic  1.98 us (2%)
    pallas_call x1, Pallas kernels, block_kernel(): pl.pallas_call(functools.partial(mlp_kernel, n, nt), out_shape=(jax.Shape...  114 us
    unnamed x2, local copies, waits for them, and re-layouts  3.59 us

profile of v2, /device:TPU:27, one launch (start us, length us, event | category | flops | bytes accessed | tf_op | source)
XLA Modules:
  0.0 121.5 jit_solution(14572172233227866692)
XLA Ops:
  0.6 0.7 fusion.3
  1.3 0.1 pad.18.clone
  1.4 0.7 pad_dynamic-slice_fusion
  2.1 1.3 %fusion.index_ref = s32[8,128]{1,0:T(8,128)} fusion(s32[1,32]{1,0:T(1,128)} %bitcast.7, s32[1,12]{1,0:T(1,128)S(1)} %fusion.3, s32[3,128]{1,0:T(4,128)S(1)} %pad_dynamic-slice_fusion, s32[8]{0:T(128)S(1)} %pad.18.clone), kind=kLoop, calls=%fused_computation.6 | loop fusion | flops 11264 | bytes 5840 | tf_op jit(solution)/shard_map/concatenate | solution.py:543
  3.4 114.5 %shard_map.185 = (bf16[128,1664]{1,0:T(8,128)(2,1)}, bf16[4,32,1664]{2,1,0:T(8,128)(2,1)}) custom-call(bf16[128,1664]{1,0:T(8,128)(2,1)} %stream_ref.1, bf16[128,1664]{1,0:T(8,128)(2,1)} %query_ref.1, bf16[128,1664]{1,0:T(8,128)(2,1)} %key_ref.1, bf16[128,1664]{1,0:T(8,128)(2,1)} %value_ref.1, s32[8,128]{1,0:T(8,128)} %fusion.index_ref, f32[1664]{0:T(1024)} %attn_gain_ref.1, ...), custom_call_target="tpu_custom_call" | custom-call | tf_op jit(solution)/shard_map/pallas_call | solution.py:448
  117.9 1.8 %copy.22 = bf16[128,1664]{1,0:T(8,128)(2,1)} copy(bf16[128,1664]{1,0:T(8,128)(2,1)} %get-tuple-element.8) | data formatting | bytes 851968
  119.7 1.8 %copy.23 = bf16[1,1,128,1664]{3,2,1,0:T(8,128)(2,1)} copy(bf16[1,1,128,1664]{3,2,1,0:T(8,128)(2,1)} %bitcast.5) | data formatting | bytes 851968
  (1 shorter events, 0.0 us)

commit v3 on v1

--- a/solution.py
+++ b/solution.py
@@ -73,6 +73,8 @@
     part,
     landed,
     total,
+    side_sum,
+    side_sem,
     outgoing,
     arrived,
     weight_sem,
@@ -246,13 +248,13 @@
             device_id_type=MESH,
         )
 
-    def partial_copy(block):
+    def partial_copy(pair, source):
         return pltpu.make_async_remote_copy(
-            src_ref=part.at[block],
-            dst_ref=landed.at[blk],
-            send_sem=rs_send.at[block],
-            recv_sem=rs_recv.at[blk],
-            device_id={"blk": block},
+            src_ref=part.at[pair],
+            dst_ref=landed.at[source],
+            send_sem=rs_send.at[pair],
+            recv_sem=rs_recv.at[source],
+            device_id={"blk": 2 * pair + lo},
             device_id_type=MESH,
         )
 
@@ -281,14 +283,11 @@
             act = (0.5 * pre * (1.0 + lax.erf(pre * 0.7071067811865476))).astype(jnp.bfloat16)
             pooled_units[:, cols] = dot(pool, act).astype(jnp.bfloat16)
         result = dot(pooled_units[...], w_proj[...]).astype(jnp.bfloat16)
-        for k in range(2):
-            part[2 * pair + k] = result[k * groups : (k + 1) * groups]
-        for k in range(2):
-            block = 2 * pair + k
-
-            @pl.when(block != blk)
-            def _(block=block):
-                partial_copy(block).start()
+        part[pair] = result.reshape(2, groups, width)
+
+        @pl.when(pair != hi)
+        def _():
+            partial_copy(pair, hi).start()
 
     def step(s, carry):
         below = hi - s
@@ -330,25 +329,29 @@
 
     lax.fori_loop(1, line + 1, step, 0)
 
-    total[...] = part[blk].astype(jnp.float32)
+    total[...] = part[hi].astype(jnp.float32)
 
     def collect(k, carry):
-        source = lax.rem(blk + k, n)
-        pltpu.make_async_remote_copy(
-            src_ref=part.at[source],
-            dst_ref=landed.at[source],
-            send_sem=rs_send.at[source],
-            recv_sem=rs_recv.at[source],
-            device_id={"blk": source},
-            device_id_type=MESH,
-        ).wait_recv()
+        source = lax.rem(hi + k, line)
+        partial_copy(source, source).wait_recv()
         total[...] += landed[source].astype(jnp.float32)
         return carry
 
-    lax.fori_loop(1, n, collect, 0)
+    lax.fori_loop(1, line, collect, 0)
+    side_sum[0] = total[1 - lo].astype(jnp.bfloat16)
+    side_copy = pltpu.make_async_remote_copy(
+        src_ref=side_sum.at[0],
+        dst_ref=side_sum.at[1],
+        send_sem=side_sem.at[0],
+        recv_sem=side_sem.at[1],
+        device_id={"blk": partner},
+        device_id_type=MESH,
+    )
+    side_copy.start()
     pool_own = pool_matrix(groups)
     own = dot(pool_own, stream_ref[...]) + dot(pool_own, att_ref[...])
-    pooled = (own + total[...]) * 0.25 + b_proj
+    side_copy.wait()
+    pooled = (own + total[lo] + side_sum[1].astype(jnp.float32)) * 0.25 + b_proj
     merge_in = layer_norm(pooled, merge_gain).astype(jnp.bfloat16)
     loads[3].wait()
     merged = (dot(merge_in, w_merge[...]) + b_merge).astype(jnp.bfloat16)
@@ -393,10 +396,10 @@
     for_sides((0, 1, 2, 3), "wait_send", True)
 
     def settle_partial(k, carry):
-        partial_copy(lax.rem(blk + k, n)).wait_send()
+        partial_copy(lax.rem(hi + k, line), hi).wait_send()
         return carry
 
-    lax.fori_loop(1, n, settle_partial, 0)
+    lax.fori_loop(1, line, settle_partial, 0)
     for k in range(1, nt):
         other = lax.rem(tok + k, nt)
         delivery(other, other).wait_recv()
@@ -452,9 +455,11 @@
             pltpu.VMEM(w_proj.shape, jnp.bfloat16),
             pltpu.VMEM(w_merge.shape, jnp.bfloat16),
             pltpu.VMEM((2 * groups, units), jnp.bfloat16),
-            pltpu.VMEM((n, groups, width), jnp.bfloat16),
-            pltpu.VMEM((n, groups, width), jnp.bfloat16),
-            pltpu.VMEM((groups, width), jnp.float32),
+            pltpu.VMEM((n // 2, 2, groups, width), jnp.bfloat16),
+            pltpu.VMEM((n // 2, 2, groups, width), jnp.bfloat16),
+            pltpu.VMEM((2, groups, width), jnp.float32),
+            pltpu.VMEM((2, groups, width), jnp.bfloat16),
+            pltpu.SemaphoreType.DMA((2,)),
             pltpu.VMEM((nt, groups, width), jnp.bfloat16),
             pltpu.VMEM((nt, groups, width), jnp.bfloat16),
             pltpu.SemaphoreType.DMA((4,)),

time: 121 us -> 118 us (0.975)
  Pallas kernels: 114 us -> 110 us
    pallas_call x1, Pallas kernels: 114 us -> 110 us  [block_kernel(): pl.pallas_call(functools.partial(mlp_kernel, n, nt), out_shape=(jax.Shape...]
where the time goes in v3:
time: 118 us; the launch traced here: 117 us
  Pallas kernels  110 us (93%)
  local copies, waits for them, and re-layouts  4.36 us (4%)
  other arithmetic  1.98 us (2%)
    pallas_call x1, Pallas kernels, block_kernel(): pl.pallas_call(functools.partial(mlp_kernel, n, nt), out_shape=(jax.Shape...  110 us
    unnamed x2, local copies, waits for them, and re-layouts  3.59 us

profile of v3, /device:TPU:27, one launch (start us, length us, event | category | flops | bytes accessed | tf_op | source)
XLA Modules:
  0.0 117.4 jit_solution(12062954329673384241)
XLA Ops:
  0.6 0.7 fusion.3
  1.3 0.1 pad.18.clone
  1.4 0.7 pad_dynamic-slice_fusion
  2.1 1.3 %fusion.index_ref = s32[8,128]{1,0:T(8,128)} fusion(s32[1,32]{1,0:T(1,128)} %bitcast.7, s32[1,12]{1,0:T(1,128)S(1)} %fusion.3, s32[3,128]{1,0:T(4,128)S(1)} %pad_dynamic-slice_fusion, s32[8]{0:T(128)S(1)} %pad.18.clone), kind=kLoop, calls=%fused_computation.6 | loop fusion | flops 11264 | bytes 5840 | tf_op jit(solution)/shard_map/concatenate | solution.py:533
  3.4 110.4 %shard_map.185 = (bf16[128,1664]{1,0:T(8,128)(2,1)}, bf16[4,32,1664]{2,1,0:T(8,128)(2,1)}) custom-call(bf16[128,1664]{1,0:T(8,128)(2,1)} %stream_ref.1, bf16[128,1664]{1,0:T(8,128)(2,1)} %query_ref.1, bf16[128,1664]{1,0:T(8,128)(2,1)} %key_ref.1, bf16[128,1664]{1,0:T(8,128)(2,1)} %value_ref.1, s32[8,128]{1,0:T(8,128)} %fusion.index_ref, f32[1664]{0:T(1024)} %attn_gain_ref.1, ...), custom_call_target="tpu_custom_call" | custom-call | tf_op jit(solution)/shard_map/pallas_call | solution.py:436
  113.8 1.8 %copy.22 = bf16[128,1664]{1,0:T(8,128)(2,1)} copy(bf16[128,1664]{1,0:T(8,128)(2,1)} %get-tuple-element.8) | data formatting | bytes 851968
  115.6 1.8 %copy.23 = bf16[1,1,128,1664]{3,2,1,0:T(8,128)(2,1)} copy(bf16[1,1,128,1664]{3,2,1,0:T(8,128)(2,1)} %bitcast.5) | data formatting | bytes 851968
  (1 shorter events, 0.0 us)

commit v4 on v3

--- a/solution.py
+++ b/solution.py
@@ -228,12 +228,22 @@
         weights = jnp.exp(scores - jnp.max(scores, axis=-1, keepdims=True))
         probs[head] = (weights / jnp.sum(weights, axis=-1, keepdims=True)).astype(jnp.bfloat16)
 
-    for_sides((3,), "wait_recv", False)
     attended[...] = jnp.zeros_like(attended)
-    for head in range(HEADS):
-        cols, mine = window(head)
-        near = values[:, :, cols].reshape(3 * rows, cols.stop - cols.start)
-        attended[:, cols] += jnp.where(mine, dot(probs[head], near), 0.0)
+
+    def attend(slot):
+        for head in range(HEADS):
+            cols, mine = window(head)
+            share = probs[head, :, slot * rows : (slot + 1) * rows]
+            attended[:, cols] += jnp.where(mine, dot(share, values[slot, :, cols]), 0.0)
+
+    attend(1)
+    for side in range(2):
+
+        @pl.when(has_below if side == 0 else has_above)
+        def _(side=side):
+            halo(side, 3).wait_recv()
+            attend(2 * side)
+
     att_ref[...] = attended[...].astype(jnp.bfloat16)
     mixed = stream_ref[...].astype(jnp.float32) + att_ref[...].astype(jnp.float32)
     gath[blk] = layer_norm(mixed, mlp_gain).astype(jnp.bfloat16)

time: 118 us -> 118 us (level)
  no operation moved by 1% of the time
where the time goes in v4:
time: 118 us
  Pallas kernels  111 us (94%)
  local copies, waits for them, and re-layouts  4.36 us (4%)
  other arithmetic  1.98 us (2%)
    pallas_call x1, Pallas kernels, block_kernel(): pl.pallas_call(functools.partial(mlp_kernel, n, nt), out_shape=(jax.Shape...  111 us
    unnamed x2, local copies, waits for them, and re-layouts  3.59 us

profile of v4, /device:TPU:27, one launch (start us, length us, event | category | flops | bytes accessed | tf_op | source)
XLA Modules:
  0.0 117.6 jit_solution(67976685022809969)
XLA Ops:
  0.6 0.7 fusion.3
  1.3 0.1 pad.18.clone
  1.4 0.7 pad_dynamic-slice_fusion
  2.1 1.3 %fusion.index_ref = s32[8,128]{1,0:T(8,128)} fusion(s32[1,32]{1,0:T(1,128)} %bitcast.7, s32[1,12]{1,0:T(1,128)S(1)} %fusion.3, s32[3,128]{1,0:T(4,128)S(1)} %pad_dynamic-slice_fusion, s32[8]{0:T(128)S(1)} %pad.18.clone), kind=kLoop, calls=%fused_computation.6 | loop fusion | flops 11264 | bytes 5840 | tf_op jit(solution)/shard_map/concatenate | solution.py:543
  3.4 110.6 %shard_map.185 = (bf16[128,1664]{1,0:T(8,128)(2,1)}, bf16[4,32,1664]{2,1,0:T(8,128)(2,1)}) custom-call(bf16[128,1664]{1,0:T(8,128)(2,1)} %stream_ref.1, bf16[128,1664]{1,0:T(8,128)(2,1)} %query_ref.1, bf16[128,1664]{1,0:T(8,128)(2,1)} %key_ref.1, bf16[128,1664]{1,0:T(8,128)(2,1)} %value_ref.1, s32[8,128]{1,0:T(8,128)} %fusion.index_ref, f32[1664]{0:T(1024)} %attn_gain_ref.1, ...), custom_call_target="tpu_custom_call" | custom-call | tf_op jit(solution)/shard_map/pallas_call | solution.py:446
  114.0 1.8 %copy.22 = bf16[128,1664]{1,0:T(8,128)(2,1)} copy(bf16[128,1664]{1,0:T(8,128)(2,1)} %get-tuple-element.8) | data formatting | bytes 851968
  115.8 1.8 %copy.23 = bf16[1,1,128,1664]{3,2,1,0:T(8,128)(2,1)} copy(bf16[1,1,128,1664]{3,2,1,0:T(8,128)(2,1)} %bitcast.5) | data formatting | bytes 851968
  (1 shorter events, 0.0 us)
